TPU v7x, 32 devices: a whole 2x2x4 slice. The times are simulated.
32 devices in a mesh: parts: 2 (over x), sta: 16 (over z, y, core).
Axes of the slice: x: 2, y: 2, z: 4, core: 2. Of those that a mesh axis runs over, the one named last changes fastest.
Arguments:
- raw_traces: bfloat16 [512, 16384], P('parts', 'sta'), parts along dimension 0, may hold values from -6 to 6
- filter_taps: bfloat16 [256], replicated, may hold values from -0.375 to 0.375
- station_order: int32 [512], P('parts'), parts along dimension 0, may hold values from 0 to 255, each once
- window_starts: int32 [32], P('parts'), parts along dimension 0, may hold values from 0 to 2048, as said below
- pairing: int32 [4, 16], replicated, may hold values from 0 to 15, as said below
Outputs:
- correlation: float32 [4, 512, 16, 256], P(None, ('parts', 'sta')), parts along dimension 1
There are 2 independent parts, one for each index of `parts`. A program takes and returns all parts, laid end to end along the dimension named above; an argument that names none is the same for every part. Nothing has to cross between parts.
Inputs may be any that keep to these rules, and one draw needn't show every extreme that they name: Each station appears once; block b holds the stations station_order[b * 16 + j], j < 16. `window_starts`: starts never fall; the first is 0 and the last is 2048; consecutive starts differ by at most 273. Row r is one round of a single round-robin tournament over the 16 blocks: pairing[r, pairing[r, b]] = b, pairing[r, b] != b, and no two rows pair the same two blocks.
All inputs are finite; a program needn't handle non-finite values.
Results may differ from a plain program's by a relative error of at most 0.0049.
Values may be sent and summed in bfloat16 or wider, within the bound.
A program may use at most 128 MiB of HBM per device.

v0:
```python
import math
import jax
import jax.numpy as jnp
from jax import lax
from jax.sharding import PartitionSpec as P

DEC = 4
TAPS = 256
SEG = 2048
BAND = 64
LAGS = 256
ROUNDS = 4
BINS = 1024


def decimate(signal, leading, filter_taps, factor):
    row_count, length = signal.shape
    outputs = length // factor
    per_tile = math.gcd(outputs, 128)
    tile_span = per_tile * factor
    margin = leading.shape[1]
    pieces = 1 + (margin + tile_span - 1) // tile_span
    tile_count = outputs // per_tile
    padded = jnp.concatenate(
        [leading, signal, jnp.zeros((row_count, (pieces - 1) * tile_span - margin), signal.dtype)],
        axis=1,
    )
    tap_count = filter_taps.shape[0]
    positions = jnp.arange(pieces * tile_span, dtype=jnp.int32)[:, None]
    column = jnp.arange(per_tile, dtype=jnp.int32)[None, :]
    tap_index = column * factor + tap_count - 1 - positions
    inside = (tap_index >= 0) & (tap_index < tap_count)
    banded = jnp.where(
        inside,
        jnp.take(filter_taps, jnp.clip(tap_index, 0, tap_count - 1)),
        jnp.zeros((), filter_taps.dtype),
    )
    summed = jnp.zeros((row_count, tile_count, per_tile), jnp.float32)
    for section_index in range(pieces):
        segment = padded[:, section_index * tile_span : section_index * tile_span + length].reshape(
            row_count, tile_count, tile_span
        )
        summed = summed + jnp.einsum(
            "rtu,ui->rti",
            segment,
            banded[section_index * tile_span : (section_index + 1) * tile_span],
            preferred_element_type=jnp.float32,
        )
    return summed.reshape(row_count, outputs)


def dft_matrix(seg_length, bin_count):
    sample = jnp.arange(seg_length, dtype=jnp.int32)
    frequency = jnp.arange(bin_count, dtype=jnp.int32)
    angles = (frequency[:, None] * sample[None, :] % seg_length).astype(jnp.float32) * (
        2.0 * math.pi / seg_length
    )
    taper_curve = 0.5 - 0.5 * jnp.cos(sample.astype(jnp.float32) * (2.0 * math.pi / seg_length))
    joined = jnp.concatenate(
        [jnp.cos(angles) * taper_curve[None, :], -jnp.sin(angles) * taper_curve[None, :]], axis=0
    )
    return joined.astype(jnp.bfloat16)


def lag_matrix(seg_length, bin_count, lag_count, window_count):
    frequency = jnp.arange(bin_count, dtype=jnp.int32)
    lag_offset = jnp.arange(lag_count, dtype=jnp.int32) - lag_count // 2 + seg_length
    angles = (frequency[:, None] * lag_offset[None, :] % seg_length).astype(jnp.float32) * (
        2.0 * math.pi / seg_length
    )
    normalizer = 1.0 / math.sqrt(bin_count * window_count)
    return jnp.stack([jnp.cos(angles) * normalizer, -jnp.sin(angles) * normalizer]).astype(
        jnp.bfloat16
    )


def whiten_flat(spectrum, band_width):
    halves, bin_count, columns = spectrum.shape
    grouped = spectrum.reshape(halves, bin_count // band_width, band_width, columns)
    band_level = jnp.sum(grouped * grouped, axis=(0, 2)) / (2 * band_width)
    scaled = grouped * (1.0 / jnp.sqrt(band_level + 1e-06))[None, :, None]
    return scaled.reshape(spectrum.shape).astype(jnp.bfloat16)


def cross_spectra(left_spec, right_spec):
    turned = jnp.stack([right_spec, jnp.stack([-right_spec[1], right_spec[0]])])
    return jnp.einsum("cfws,kcfwt->kfst", left_spec, turned, preferred_element_type=jnp.float32)


def body(raw_traces, filter_taps, station_order, window_starts, pairing):
    members = lax.axis_size("sta")
    station_count, local_time = raw_traces.shape
    block_size = station_count // members
    margin = TAPS - DEC
    ordered = jnp.take(raw_traces, station_order, axis=0)
    gathered = lax.all_to_all(ordered, "sta", split_axis=0, concat_axis=1, tiled=True)
    leading = jnp.zeros((block_size, margin), gathered.dtype)
    low_rate = decimate(gathered, leading, filter_taps, DEC).astype(jnp.bfloat16)
    window_count = window_starts.shape[0]
    windows = jax.vmap(
        lambda first_sample: lax.dynamic_slice_in_dim(low_rate, first_sample, SEG, 1)
    )(window_starts)
    windows = windows.reshape(window_count * block_size, SEG)
    spectrum = lax.dot_general(
        dft_matrix(SEG, BINS), windows, (((1,), (1,)), ((), ())), preferred_element_type=jnp.float32
    )
    whitened = whiten_flat(spectrum.reshape(2, BINS, window_count * block_size), BAND)
    by_bin = lax.all_to_all(whitened[None], "sta", split_axis=2, concat_axis=0, tiled=True)
    lag_table = lag_matrix(SEG, BINS, LAGS, window_count)
    own_spec = whitened.reshape(2, BINS, window_count, block_size)
    collected = []
    for round_index in range(ROUNDS):
        picked = jnp.take(by_bin, pairing[round_index], axis=0)
        partner_spec = lax.all_to_all(picked, "sta", split_axis=0, concat_axis=2, tiled=True)
        partner_spec = partner_spec.reshape(2, BINS, window_count, block_size)
        cross_spec = cross_spectra(own_spec, partner_spec).astype(jnp.bfloat16)
        collected.append(cross_spec.reshape(2, BINS, block_size * block_size))
    correlated = jnp.einsum(
        "rkfp,kfl->rpl", jnp.stack(collected), lag_table, preferred_element_type=jnp.float32
    )
    return correlated.reshape(ROUNDS, block_size, block_size, LAGS)


def solution(mesh):
    return jax.shard_map(
        body,
        mesh=mesh,
        in_specs=(P("parts", "sta"), P(), P("parts"), P("parts"), P()),
        out_specs=P(None, ("parts", "sta"), None, None),
        check_vma=False,
    )
```

profile of v0, /device:TPU:0, one launch (start us, length us, event | category | flops | bytes accessed | tf_op | source)
XLA Modules:
  0.0 1280.5 jit_solution(12925101330786375420)
XLA Ops:
  3.6 7.4 all-to-all-start
  11.3 35.5 %multiply_convert_fusion.1 = (bf16[1024,2048]{1,0:T(8,128)(2,1)}, bf16[1024,2048]{1,0:T(8,128)(2,1)}) fusion(f32[2048]{0:T(1024)S(1)} %multiply_subtract_fusion), kind=kLoop, calls=%fused_computation.20 | loop fusion | flops 39845888 | bytes 8396800 | tf_op jit(solution)/shard_map/convert.2
  46.8 764.8 %gather_fusion.1 = bf16[131072]{0:T(1024)(128)(2,1)S(1)} fusion(bf16[256]{0:T(256)(128)(2,1)S(1)} %copy-done.2, s32[131072]{0:T(1024)S(1)} %fusion.28), kind=kCustom, calls=%fused_computation.5 | custom fusion | bytes 1048576 | tf_op jit(solution)/shard_map/jit(_take)/gather | solution.py:35
  812.0 8.4 pad_maximum_fusion
  821.7 21.5 %while.1 = (s32[]{:T(128)}, bf16[16,4096]{1,0:T(8,128)(2,1)S(1)}, s32[16,2]{0,1:T(2,128)S(1)}, bf16[16,16,2048]{2,1,0:T(8,128)(2,1)S(1)}, s32[]{:T(128)}) while((s32[]{:T(128)}, bf16[16,4096]{1,0:T(8,128)(2,1)S(1)}, s32[16,2]{0,1:T(2,128)S(1)}, bf16[16,16,2048]{2,1,0:T(8,128)(2,1)S(1)}, s32[]{:T(128)}) %tuple.38), condition=%wide.while_cond, body=%wide.while_body.sunk | while | flops 2 | bytes 131169 | solution.py:101
  843.3 5.8 multiply_reduce_fusion
  849.3 2.1 copy.103
  851.4 6.0 all-to-all-start.1
  857.5 22.9 %all-to-all-done.1 = bf16[1,2,1024,256]{3,1,0,2:T(2,128)(2,1)S(1)} async-done(((bf16[1,2,1024,256]{3,1,0,2:T(2,128)(2,1)}), bf16[1,2,1024,256]{3,1,0,2:T(2,128)(2,1)S(1)}, u32[]{:S(2)}, u32[]{:S(2)}) %all-to-all-start.1) | async-done | bytes 1048608 | tf_op jit(solution)/shard_map/all_to_all | solution.py:108
  882.7 1.6 gather_fusion.2
  884.3 2.3 broadcast_select_fusion.3
  886.7 6.9 all-to-all-start.2
  893.6 1.6 gather_fusion.3
  895.2 2.4 broadcast_select_fusion.2
  897.6 19.0 %all-to-all-done.2 = bf16[16,2,64,256]{3,2,1,0:T(8,128)(2,1)} async-done(((bf16[16,2,64,256]{3,2,1,0:T(8,128)(2,1)}), bf16[16,2,64,256]{3,2,1,0:T(8,128)(2,1)}, u32[]{:S(2)}, u32[]{:S(2)}) %all-to-all-start.2) | async-done | bytes 1048608 | tf_op jit(solution)/shard_map/all_to_all | solution.py:114
  916.6 7.2 all-to-all-start.3
  923.8 1.6 gather_fusion.4
  925.4 2.3 broadcast_select_fusion.1
  927.7 19.0 %all-to-all-done.3 = bf16[16,2,64,256]{3,2,1,0:T(8,128)(2,1)} async-done(((bf16[16,2,64,256]{3,2,1,0:T(8,128)(2,1)}), bf16[16,2,64,256]{3,2,1,0:T(8,128)(2,1)}, u32[]{:S(2)}, u32[]{:S(2)}) %all-to-all-start.3) | async-done | bytes 1048608 | tf_op jit(solution)/shard_map/all_to_all | solution.py:114
  946.8 6.9 all-to-all-start.4
  953.7 1.6 gather_fusion.5
  955.3 2.4 broadcast_select_fusion
  957.6 19.0 %all-to-all-done.4 = bf16[16,2,64,256]{3,2,1,0:T(8,128)(2,1)} async-done(((bf16[16,2,64,256]{3,2,1,0:T(8,128)(2,1)}), bf16[16,2,64,256]{3,2,1,0:T(8,128)(2,1)}, u32[]{:S(2)}, u32[]{:S(2)}) %all-to-all-start.4) | async-done | bytes 1048608 | tf_op jit(solution)/shard_map/all_to_all | solution.py:114
  976.7 6.9 all-to-all-start.5
  983.6 5.5 multiply_convert_fusion.4
  989.0 2.8 copy.109
  991.8 3.2 convert_element_type.96
  995.1 12.1 copy.132
  1007.2 3.8 copy.106
  1011.0 3.8 copy.113
  1014.8 3.8 copy.119
  1019.9 2.3 slice_negate_fusion.2
  1022.2 2.2 slice_negate_fusion.1
  1024.5 2.8 copy.125
  1030.7 4.1 stack_reshape.24
  1036.3 32.0 %copy.110 = bf16[2,2,1024,16,16]{3,4,1,0,2:T(8,128)(2,1)} copy(bf16[2,2,1024,16,16]{2,4,3,1,0:T(8,128)(2,1)S(1)} %pad_maximum_fusion.1) | data formatting | bytes 4194304 | tf_op jit(solution)/shard_map/stack | solution.py:86
  1068.3 13.4 %fusion.6 = bf16[2,1024,16,16]{2,3,0,1:T(8,128)(2,1)} fusion(bf16[2,2,1024,16,16]{3,4,1,0,2:T(8,128)(2,1)} %copy.110, bf16[2,1024,16,16,1]{3,2,0,4,1:T(8,128)(2,1)} %copy.132), kind=kOutput, calls=%fused_computation.24 | convolution fusion | flops 34078720 | bytes 4194304 | tf_op jit(solution)/shard_map/cfws,kcfwt->kfst/dot_general | solution.py:87
  1081.7 10.1 copy.112
  1091.8 2.9 copy.114
  1094.7 2.6 neg.69
  1097.3 2.9 copy.115
  1100.2 2.6 slice.77
  1102.9 2.2 stack_reshape.26
  1107.8 23.2 %copy.116 = bf16[2,2,1024,16,16]{3,4,1,0,2:T(8,128)(2,1)} copy(bf16[2,2,1024,16,16]{2,4,3,1,0:T(8,128)(2,1)S(1)} %pad_maximum_fusion.2) | data formatting | bytes 4194304 | tf_op jit(solution)/shard_map/stack | solution.py:86
  1131.1 13.4 %fusion.7 = bf16[2,1024,16,16]{2,3,0,1:T(8,128)(2,1)} fusion(bf16[2,2,1024,16,16]{3,4,1,0,2:T(8,128)(2,1)} %copy.116, bf16[2,1024,16,16,1]{3,2,0,4,1:T(8,128)(2,1)} %copy.132), kind=kOutput, calls=%fused_computation.25 | convolution fusion | flops 34078720 | bytes 4194304 | tf_op jit(solution)/shard_map/cfws,kcfwt->kfst/dot_general | solution.py:87
  1144.5 10.3 copy.118
  1154.8 2.9 copy.120
  1157.7 2.6 neg.71
  1160.3 2.9 copy.121
  1163.2 2.6 slice.81
  1165.8 2.2 stack_reshape.28
  1169.3 1.4 pad_maximum_fusion.3
  1170.8 23.2 %copy.122 = bf16[2,2,1024,16,16]{3,4,1,0,2:T(8,128)(2,1)} copy(bf16[2,2,1024,16,16]{2,4,3,1,0:T(8,128)(2,1)S(1)} %pad_maximum_fusion.3) | data formatting | bytes 4194304 | tf_op jit(solution)/shard_map/stack | solution.py:86
  1194.0 13.4 %fusion.8 = bf16[2,1024,16,16]{2,3,0,1:T(8,128)(2,1)} fusion(bf16[2,2,1024,16,16]{3,4,1,0,2:T(8,128)(2,1)} %copy.122, bf16[2,1024,16,16,1]{3,2,0,4,1:T(8,128)(2,1)} %copy.132), kind=kOutput, calls=%fused_computation.26 | convolution fusion | flops 34078720 | bytes 4194304 | tf_op jit(solution)/shard_map/cfws,kcfwt->kfst/dot_general | solution.py:87
  1207.4 10.2 copy.124
  1217.6 1.9 copy.126
  1219.4 1.9 neg.73
  1221.4 1.9 copy.127
  1223.2 1.9 slice.85
  1225.2 2.5 stack_reshape.30
  1229.2 23.2 %copy.128 = bf16[2,2,1024,16,16]{3,4,1,0,2:T(8,128)(2,1)} copy(bf16[2,2,1024,16,16]{2,4,3,1,0:T(8,128)(2,1)S(1)} %pad_maximum_fusion.4) | data formatting | bytes 4194304 | tf_op jit(solution)/shard_map/stack | solution.py:86
  1252.5 13.4 %fusion.9 = bf16[2,1024,16,16]{2,3,0,1:T(8,128)(2,1)} fusion(bf16[2,2,1024,16,16]{3,4,1,0,2:T(8,128)(2,1)} %copy.128, bf16[2,1024,16,16,1]{3,2,0,4,1:T(8,128)(2,1)} %copy.132), kind=kOutput, calls=%fused_computation.27 | convolution fusion | flops 34078720 | bytes 4194304 | tf_op jit(solution)/shard_map/cfws,kcfwt->kfst/dot_general | solution.py:87
  1265.9 10.1 copy.130
  1276.1 4.0 fusion.10
  (116 shorter events, 41.2 us)
Async XLA Ops:
  0.0 1.5 copy-start
  0.0 46.8 %copy-start.11 = (s32[16]{0:T(128)S(1)}, s32[16]{0:T(128)}, u32[]{:S(2)}) copy-start(s32[16]{0:T(128)} %param.10) | copy-start | bytes 196
  0.0 46.8 %copy-start.2 = (bf16[256]{0:T(256)(128)(2,1)S(1)}, bf16[256]{0:T(256)(128)(2,1)}, u32[]{:S(2)}) copy-start(bf16[256]{0:T(256)(128)(2,1)} %param.8) | copy-start | bytes 1540
  3.6 816.7 %all-to-all-start = ((bf16[16,16,1024]{2,1,0:T(8,128)(2,1)}), bf16[16,16,1024]{2,1,0:T(8,128)(2,1)S(1)}, u32[]{:S(2)}, u32[]{:S(2)}) async-start(bf16[16,16,1024]{2,1,0:T(8,128)(2,1)} %broadcast_select_fusion.4), calls=%async_computation | async-start | bytes 1048576 | tf_op jit(solution)/shard_map/all_to_all | solution.py:96
  843.3 14.2 %copy-start.10 = (s32[4,16]{1,0:T(4,128)S(1)}, s32[4,16]{1,0:T(4,128)}, u32[]{:S(2)}) copy-start(s32[4,16]{1,0:T(4,128)} %param.11) | copy-start | bytes 772
  851.4 29.0 %all-to-all-start.1 = ((bf16[1,2,1024,256]{3,1,0,2:T(2,128)(2,1)}), bf16[1,2,1024,256]{3,1,0,2:T(2,128)(2,1)S(1)}, u32[]{:S(2)}, u32[]{:S(2)}) async-start(bf16[1,2,1024,256]{3,1,0,2:T(2,128)(2,1)} %copy.103), calls=%async_computation.1 | async-start | bytes 2097152 | tf_op jit(solution)/shard_map/all_to_all | solution.py:108
  880.4 1.0 copy-start.6
  886.7 29.9 %all-to-all-start.2 = ((bf16[16,2,64,256]{3,2,1,0:T(8,128)(2,1)}), bf16[16,2,64,256]{3,2,1,0:T(8,128)(2,1)}, u32[]{:S(2)}, u32[]{:S(2)}) async-start(bf16[16,2,64,256]{3,2,1,0:T(8,128)(2,1)} %broadcast_select_fusion.3), calls=%async_computation.2 | async-start | bytes 2097152 | tf_op jit(solution)/shard_map/all_to_all | solution.py:114
  916.6 30.2 %all-to-all-start.3 = ((bf16[16,2,64,256]{3,2,1,0:T(8,128)(2,1)}), bf16[16,2,64,256]{3,2,1,0:T(8,128)(2,1)}, u32[]{:S(2)}, u32[]{:S(2)}) async-start(bf16[16,2,64,256]{3,2,1,0:T(8,128)(2,1)} %broadcast_select_fusion.2), calls=%async_computation.3 | async-start | bytes 2097152 | tf_op jit(solution)/shard_map/all_to_all | solution.py:114
  946.8 29.9 %all-to-all-start.4 = ((bf16[16,2,64,256]{3,2,1,0:T(8,128)(2,1)}), bf16[16,2,64,256]{3,2,1,0:T(8,128)(2,1)}, u32[]{:S(2)}, u32[]{:S(2)}) async-start(bf16[16,2,64,256]{3,2,1,0:T(8,128)(2,1)} %broadcast_select_fusion.1), calls=%async_computation.4 | async-start | bytes 2097152 | tf_op jit(solution)/shard_map/all_to_all | solution.py:114
  976.7 47.8 %all-to-all-start.5 = ((bf16[16,2,64,256]{3,2,1,0:T(8,128)(2,1)}), bf16[16,2,64,256]{3,2,1,0:T(8,128)(2,1)S(1)}, u32[]{:S(2)}, u32[]{:S(2)}) async-start(bf16[16,2,64,256]{3,2,1,0:T(8,128)(2,1)} %broadcast_select_fusion), calls=%async_computation.5 | async-start | bytes 2097152 | tf_op jit(solution)/shard_map/all_to_all | solution.py:114
  1081.7 21.1 %copy-start.5 = (bf16[1,2,16,64,256]{3,2,4,1,0:T(8,128)(2,1)S(1)}, bf16[1,2,16,64,256]{3,2,4,1,0:T(8,128)(2,1)}, u32[]{:S(2)}) copy-start(bf16[1,2,16,64,256]{3,2,4,1,0:T(8,128)(2,1)} %copy.113) | copy-start | bytes 3145732
  1144.5 21.3 %copy-start.4 = (bf16[1,2,16,64,256]{3,2,4,1,0:T(8,128)(2,1)S(1)}, bf16[1,2,16,64,256]{3,2,4,1,0:T(8,128)(2,1)}, u32[]{:S(2)}) copy-start(bf16[1,2,16,64,256]{3,2,4,1,0:T(8,128)(2,1)} %copy.119) | copy-start | bytes 3145732
  1207.4 17.8 %copy-start.3 = (bf16[1,2,16,64,256]{3,2,4,1,0:T(8,128)(2,1)S(1)}, bf16[1,2,16,64,256]{3,2,4,1,0:T(8,128)(2,1)}, u32[]{:S(2)}) copy-start(bf16[1,2,16,64,256]{3,2,4,1,0:T(8,128)(2,1)} %copy.125) | copy-start | bytes 3145732
  1265.9 10.1 copy-start.7
  1265.9 10.1 copy-start.8
  1265.9 10.1 copy-start.9
  1276.0 4.0 copy-start.1
where the time goes:
time: 1290 us; the launch traced here: 1280 us
  local copies, waits for them, and re-layouts  1020 us (79%)
  waiting for transfers between devices  80 us (6%)
  other arithmetic  76.3 us (6%)
  matrix products  64.1 us (5%)
  starting transfers between devices  41.3 us (3%)
    gather x1, local copies, waits for them, and re-layouts, decimate(): jnp.take(filter_taps, jnp.clip(tap_index, 0, tap_count - 1))  765 us
    another operation x8, local copies, waits for them, and re-layouts, cross_spectra(): turned = jnp.stack([right_spec, jnp.stack([-right_spec[1], right_spec[0]])])  113 us
    all_to_all x4, waiting for transfers between devices, body(): lax.all_to_all(picked, 'sta', split_axis=0, concat_axis=2, tiled=True)  57.1 us
    dot_general x4, matrix products, cross_spectra(): jnp.einsum('cfws,kcfwt->kfst', left_spec, turned, preferred_element_type=...  53.7 us
    another operation x2, other arithmetic  41 us
    convert_element_type x4, local copies, waits for them, and re-layouts, body(): cross_spec = cross_spectra(own_spec, partner_spec).astype(jnp.bfloat16)  40.7 us
    all_to_all x4, starting transfers between devices, body(): lax.all_to_all(picked, 'sta', split_axis=0, concat_axis=2, tiled=True)  27.9 us
  transfers between devices with their start and end apart: 6, of which 4 were waited for; matrix products, arithmetic and copies ran while one was open for 67% of the time, Pallas kernels for 0%

commit v1 on v0

--- a/solution.py
+++ b/solution.py
@@ -3,6 +3,7 @@
 import jax.numpy as jnp
 from jax import lax
 from jax.sharding import PartitionSpec as P
+from jax.lax import axis_index, axis_size, ppermute
 
 DEC = 4
 TAPS = 256
@@ -11,6 +12,22 @@
 LAGS = 256
 ROUNDS = 4
 BINS = 1024
+
+
+def direct_bench_on(block_in, k_dim, x_local):
+    mixed_arr = block_in.shape
+    side_arr = block_in.reshape(
+        *mixed_arr[:k_dim], x_local, mixed_arr[k_dim] // x_local, *mixed_arr[k_dim + 1 :]
+    )
+    b_next = jnp.moveaxis(side_arr, k_dim, 0)
+    return b_next
+
+
+def place_packet_all(state, ndim_at):
+    fresh = list(state.shape[1:])
+    fresh[ndim_at] *= state.shape[0]
+    arr_now = jnp.moveaxis(state, 0, ndim_at).reshape(fresh)
+    return arr_now
 
 
 def decimate(signal, leading, filter_taps, factor):
@@ -111,7 +128,14 @@
     collected = []
     for round_index in range(ROUNDS):
         picked = jnp.take(by_bin, pairing[round_index], axis=0)
-        partner_spec = lax.all_to_all(picked, "sta", split_axis=0, concat_axis=2, tiled=True)
+        current_block, r1 = (axis_size("sta"), axis_index("sta"))
+        prior = direct_bench_on(picked, 0, current_block)
+        pile = [prior[r1]]
+        for j0 in [*range(1, current_block)]:
+            left_arr = prior[r1 ^ j0]
+            pile.append(ppermute(left_arr, "sta", [(rr, rr ^ j0) for rr in range(current_block)]))
+        prior = jnp.stack(pile, axis=0)[r1 ^ jnp.arange(current_block)]
+        partner_spec = place_packet_all(prior, 2)
         partner_spec = partner_spec.reshape(2, BINS, window_count, block_size)
         cross_spec = cross_spectra(own_spec, partner_spec).astype(jnp.bfloat16)
         collected.append(cross_spec.reshape(2, BINS, block_size * block_size))

time: 1290 us -> 1300 us (level)
  waiting for transfers between devices: 80 us -> 0.16 us
  starting transfers between devices: 41.3 us -> 100 us
  local copies, waits for them, and re-layouts: 1020 us -> 1060 us
    ppermute x0 -> x60, starting transfers between devices: none -> 86.4 us  [body(): ppermute(left_arr, 'sta', [(rr, rr ^ j0) for rr in range(current_block)])]
    all_to_all x4 -> x0, waiting for transfers between devices: 57.1 us -> none  [body(): lax.all_to_all(picked, 'sta', split_axis=0, concat_axis=2, tiled=True)]
    unnamed x27 -> x97, local copies, waits for them, and re-layouts: 1.38 us -> 50 us
    all_to_all x4 -> x0, starting transfers between devices: 27.9 us -> none  [body(): lax.all_to_all(picked, 'sta', split_axis=0, concat_axis=2, tiled=True)]
    all_to_all x1, waiting for transfers between devices: 22.9 us -> 0.01 us  [body(): lax.all_to_all(whitened[None], 'sta', split_axis=2, concat_axis=0, tiled=...]
    all_to_all x4 -> x0, local copies, waits for them, and re-layouts: 14.3 us -> none  [body(): lax.all_to_all(picked, 'sta', split_axis=0, concat_axis=2, tiled=True)]
    gather x48 -> x52, local copies, waits for them, and re-layouts: 21.2 us -> 29.5 us
  transfers between devices with their start and end apart: 6 -> 62, of which waited for: 4 -> 0; matrix products, arithmetic and copies ran while one was open for 67% -> 70% of each run, Pallas kernels for 0% -> 0%
where the time goes in v1:
time: 1300 us; the launch traced here: 1290 us
  local copies, waits for them, and re-layouts  1060 us (82%)
  starting transfers between devices  100 us (8%)
  other arithmetic  65 us (5%)
  matrix products  63.8 us (5%)
    gather x1, local copies, waits for them, and re-layouts, decimate(): jnp.take(filter_taps, jnp.clip(tap_index, 0, tap_count - 1))  765 us
    another operation x8, local copies, waits for them, and re-layouts, cross_spectra(): turned = jnp.stack([right_spec, jnp.stack([-right_spec[1], right_spec[0]])])  104 us
    ppermute x60, starting transfers between devices, body(): ppermute(left_arr, 'sta', [(rr, rr ^ j0) for rr in range(current_block)])  86.4 us
    dot_general x4, matrix products, cross_spectra(): jnp.einsum('cfws,kcfwt->kfst', left_spec, turned, preferred_element_type=...  53.5 us
    unnamed x97, local copies, waits for them, and re-layouts  50 us
    another operation x2, other arithmetic  41 us
    convert_element_type x4, local copies, waits for them, and re-layouts, body(): cross_spec = cross_spectra(own_spec, partner_spec).astype(jnp.bfloat16)  40.6 us
  transfers between devices with their start and end apart: 62, of which 0 were waited for; matrix products, arithmetic and copies ran while one was open for 70% of the time, Pallas kernels for 0%

profile of v1, /device:TPU:0, one launch (start us, length us, event | category | flops | bytes accessed | tf_op | source)
XLA Modules:
  0.0 1289.8 jit_solution(13758428329623981596)
XLA Ops:
  3.6 7.4 all-to-all-start
  11.3 35.5 %multiply_convert_fusion.1 = (bf16[1024,2048]{1,0:T(8,128)(2,1)}, bf16[1024,2048]{1,0:T(8,128)(2,1)}) fusion(f32[2048]{0:T(1024)S(1)} %multiply_subtract_fusion), kind=kLoop, calls=%fused_computation.24 | loop fusion | flops 39845888 | bytes 8396800 | tf_op jit(solution)/shard_map/convert.2
  46.9 764.8 %gather_fusion.1 = bf16[131072]{0:T(1024)(128)(2,1)S(1)} fusion(bf16[256]{0:T(256)(128)(2,1)S(1)} %copy-done.2, s32[131072]{0:T(1024)S(1)} %fusion.28), kind=kCustom, calls=%fused_computation.5 | custom fusion | bytes 1048576 | tf_op jit(solution)/shard_map/jit(_take)/gather | solution.py:52
  812.0 8.5 pad_maximum_fusion
  821.8 21.5 %while.1 = (s32[]{:T(128)}, bf16[16,4096]{1,0:T(8,128)(2,1)S(1)}, s32[16,2]{0,1:T(2,128)S(1)}, bf16[16,16,2048]{2,1,0:T(8,128)(2,1)S(1)}, s32[]{:T(128)}) while((s32[]{:T(128)}, bf16[16,4096]{1,0:T(8,128)(2,1)S(1)}, s32[16,2]{0,1:T(2,128)S(1)}, bf16[16,16,2048]{2,1,0:T(8,128)(2,1)S(1)}, s32[]{:T(128)}) %tuple.96), condition=%wide.while_cond, body=%wide.while_body.sunk | while | flops 2 | bytes 131169 | solution.py:118
  843.3 5.8 multiply_reduce_fusion
  849.4 2.1 copy.234
  851.5 6.2 all-to-all-start.1
  857.9 5.5 multiply_convert_fusion.4
  863.4 2.8 copy.240
  866.2 3.2 convert_element_type.96
  869.5 12.1 copy.263
  892.6 2.4 collective-permute-start.3
  897.6 2.6 collective-permute-start.5
  903.2 2.9 collective-permute-start.7
  909.0 2.3 collective-permute-start.9
  913.6 2.5 collective-permute-start.11
  918.7 3.2 collective-permute-start.13
  928.0 2.3 collective-permute-start.18
  933.6 2.0 collective-permute-start.20
  937.5 2.2 collective-permute-start.22
  941.5 2.4 collective-permute-start.24
  946.2 2.5 collective-permute-start.26
  951.1 3.0 collective-permute-start.28
  960.7 3.7 collective-permute-start.33
  971.3 1.9 collective-permute-start.36
  974.7 2.1 collective-permute-start.37
  982.9 2.4 collective-permute-start.40
  990.7 2.3 collective-permute-start.43
  993.6 2.2 collective-permute-start.44
  1000.2 2.0 collective-permute-start.48
  1003.5 2.8 gather_fusion.4
  1006.3 2.2 slice_negate_fusion.1
  1013.9 2.0 collective-permute-start.52
  1022.3 2.2 collective-permute-start.55
  1025.2 1.9 collective-permute-start.56
  1030.2 2.6 collective-permute-start.58
  1038.3 3.2 copy.237
  1041.5 2.8 copy.244
  1044.3 3.8 copy.250
  1051.7 2.9 copy.256
  1057.9 4.1 stack_reshape_reshape.12
  1063.5 23.3 %copy.241 = bf16[2,2,1024,16,16]{3,4,1,0,2:T(8,128)(2,1)} copy(bf16[2,2,1024,16,16]{2,4,3,1,0:T(8,128)(2,1)S(1)} %pad_maximum_fusion.1) | data formatting | bytes 4194304 | tf_op jit(solution)/shard_map/stack | solution.py:103
  1086.8 13.4 %fusion.6 = bf16[2,1024,16,16]{2,3,0,1:T(8,128)(2,1)} fusion(bf16[2,2,1024,16,16]{3,4,1,0,2:T(8,128)(2,1)} %copy.241, bf16[2,1024,16,16,1]{3,2,0,4,1:T(8,128)(2,1)} %copy.263), kind=kOutput, calls=%fused_computation.28 | convolution fusion | flops 34078720 | bytes 4194304 | tf_op jit(solution)/shard_map/cfws,kcfwt->kfst/dot_general | solution.py:104
  1100.2 10.3 copy.243
  1112.3 1.9 neg.69
  1116.2 1.9 slice.77
  1118.1 2.3 stack_reshape_reshape.13
  1121.9 23.3 %copy.247 = bf16[2,2,1024,16,16]{3,4,1,0,2:T(8,128)(2,1)} copy(bf16[2,2,1024,16,16]{2,4,3,1,0:T(8,128)(2,1)S(1)} %pad_maximum_fusion.2) | data formatting | bytes 4194304 | tf_op jit(solution)/shard_map/stack | solution.py:103
  1145.2 13.4 %fusion.7 = bf16[2,1024,16,16]{2,3,0,1:T(8,128)(2,1)} fusion(bf16[2,2,1024,16,16]{3,4,1,0,2:T(8,128)(2,1)} %copy.247, bf16[2,1024,16,16,1]{3,2,0,4,1:T(8,128)(2,1)} %copy.263), kind=kOutput, calls=%fused_computation.29 | convolution fusion | flops 34078720 | bytes 4194304 | tf_op jit(solution)/shard_map/cfws,kcfwt->kfst/dot_general | solution.py:104
  1158.6 10.1 copy.249
  1170.6 1.9 neg.71
  1174.4 1.9 slice.81
  1176.4 2.5 stack_reshape_reshape.14
  1180.4 23.3 %copy.253 = bf16[2,2,1024,16,16]{3,4,1,0,2:T(8,128)(2,1)} copy(bf16[2,2,1024,16,16]{2,4,3,1,0:T(8,128)(2,1)S(1)} %pad_maximum_fusion.3) | data formatting | bytes 4194304 | tf_op jit(solution)/shard_map/stack | solution.py:103
  1203.7 13.4 %fusion.8 = bf16[2,1024,16,16]{2,3,0,1:T(8,128)(2,1)} fusion(bf16[2,2,1024,16,16]{3,4,1,0,2:T(8,128)(2,1)} %copy.253, bf16[2,1024,16,16,1]{3,2,0,4,1:T(8,128)(2,1)} %copy.263), kind=kOutput, calls=%fused_computation.30 | convolution fusion | flops 34078720 | bytes 4194304 | tf_op jit(solution)/shard_map/cfws,kcfwt->kfst/dot_general | solution.py:104
  1217.0 10.1 copy.255
  1229.0 1.9 neg.73
  1232.8 1.9 slice.85
  1234.8 2.3 stack_reshape_reshape.15
  1238.6 23.3 %copy.259 = bf16[2,2,1024,16,16]{3,4,1,0,2:T(8,128)(2,1)} copy(bf16[2,2,1024,16,16]{2,4,3,1,0:T(8,128)(2,1)S(1)} %pad_maximum_fusion.4) | data formatting | bytes 4194304 | tf_op jit(solution)/shard_map/stack | solution.py:103
  1261.9 13.4 %fusion.9 = bf16[2,1024,16,16]{2,3,0,1:T(8,128)(2,1)} fusion(bf16[2,2,1024,16,16]{3,4,1,0,2:T(8,128)(2,1)} %copy.259, bf16[2,1024,16,16,1]{3,2,0,4,1:T(8,128)(2,1)} %copy.263), kind=kOutput, calls=%fused_computation.31 | convolution fusion | flops 34078720 | bytes 4194304 | tf_op jit(solution)/shard_map/cfws,kcfwt->kfst/dot_general | solution.py:104
  1275.3 10.1 copy.261
  1285.4 4.0 fusion.10
  (310 shorter events, 146.7 us)
Async XLA Ops:
  0.0 46.8 %copy-start.16 = (s32[16]{0:T(128)S(1)}, s32[16]{0:T(128)}, u32[]{:S(2)}) copy-start(s32[16]{0:T(128)} %param.10) | copy-start | bytes 196
  0.0 46.8 %copy-start.2 = (bf16[256]{0:T(256)(128)(2,1)S(1)}, bf16[256]{0:T(256)(128)(2,1)}, u32[]{:S(2)}) copy-start(bf16[256]{0:T(256)(128)(2,1)} %param.8) | copy-start | bytes 1540
  3.6 816.8 %all-to-all-start = ((bf16[16,16,1024]{2,1,0:T(8,128)(2,1)}), bf16[16,16,1024]{2,1,0:T(8,128)(2,1)S(1)}, u32[]{:S(2)}, u32[]{:S(2)}) async-start(bf16[16,16,1024]{2,1,0:T(8,128)(2,1)} %broadcast_select_fusion.4), calls=%async_computation | async-start | bytes 1048576 | tf_op jit(solution)/shard_map/all_to_all | solution.py:113
  851.5 30.0 %all-to-all-start.1 = ((bf16[1,2,1024,256]{3,1,0,2:T(2,128)(2,1)}), bf16[1,2,1024,256]{3,1,0,2:T(2,128)(2,1)S(1)}, u32[]{:S(2)}, u32[]{:S(2)}) async-start(bf16[1,2,1024,256]{3,1,0,2:T(2,128)(2,1)} %copy.234), calls=%async_computation.1 | async-start | bytes 2097152 | tf_op jit(solution)/shard_map/all_to_all | solution.py:125
  890.4 7.2 collective-permute-start
  890.9 10.8 collective-permute-start.1
  892.6 10.6 collective-permute-start.2
  892.6 15.0 %collective-permute-start.3 = (bf16[1,2,64,256]{3,2,1,0:T(8,128)(2,1)S(1)}, bf16[1,2,64,256]{3,2,1,0:T(8,128)(2,1)}, u32[]{:S(2)}, u32[]{:S(2)}) collective-permute-start(bf16[1,2,64,256]{3,2,1,0:T(8,128)(2,1)S(1)} %get-tuple-element.43), channel_id=1, source_target_pairs={{0,4},{1,5},{2,6},{3,7},{4,0},{5,1},{6,2},{7,3},{8,12},{9,13},{10,... | collective-permute-start | bytes 196616 | tf_op jit(solution)/shard_map/ppermute | solution.py:136
  895.0 14.0 %collective-permute-start.4 = (bf16[1,2,64,256]{3,2,1,0:T(8,128)(2,1)S(1)}, bf16[1,2,64,256]{3,2,1,0:T(8,128)(2,1)S(1)}, u32[]{:S(2)}, u32[]{:S(2)}) collective-permute-start(bf16[1,2,64,256]{3,2,1,0:T(8,128)(2,1)S(1)} %get-tuple-element.42), channel_id=1, source_target_pairs={{0,5},{1,4},{2,7},{3,6},{4,1},{5,0},{6,3},{7,2},{8,13},{9,12},{10,... | collective-permute-start | bytes 196616 | tf_op jit(solution)/shard_map/ppermute | solution.py:136
  897.6 14.4 %collective-permute-start.5 = (bf16[1,2,64,256]{3,2,1,0:T(8,128)(2,1)S(1)}, bf16[1,2,64,256]{3,2,1,0:T(8,128)(2,1)S(1)}, u32[]{:S(2)}, u32[]{:S(2)}) collective-permute-start(bf16[1,2,64,256]{3,2,1,0:T(8,128)(2,1)S(1)} %get-tuple-element.41), channel_id=1, source_target_pairs={{0,6},{1,7},{2,4},{3,5},{4,2},{5,3},{6,0},{7,1},{8,14},{9,15},{10,... | collective-permute-start | bytes 196616 | tf_op jit(solution)/shard_map/ppermute | solution.py:136
  901.7 11.9 collective-permute-start.6
  903.2 13.6 %collective-permute-start.7 = (bf16[1,2,64,256]{3,2,1,0:T(8,128)(2,1)S(1)}, bf16[1,2,64,256]{3,2,1,0:T(8,128)(2,1)S(1)}, u32[]{:S(2)}, u32[]{:S(2)}) collective-permute-start(bf16[1,2,64,256]{3,2,1,0:T(8,128)(2,1)S(1)} %get-tuple-element.39), channel_id=1, source_target_pairs={{0,8},{1,9},{2,10},{3,11},{4,12},{5,13},{6,14},{7,15},{8,0},{9,1},... | collective-permute-start | bytes 196616 | tf_op jit(solution)/shard_map/ppermute | solution.py:136
  907.6 11.1 collective-permute-start.8
  909.0 13.5 %collective-permute-start.9 = (bf16[1,2,64,256]{3,2,1,0:T(8,128)(2,1)S(1)}, bf16[1,2,64,256]{3,2,1,0:T(8,128)(2,1)S(1)}, u32[]{:S(2)}, u32[]{:S(2)}) collective-permute-start(bf16[1,2,64,256]{3,2,1,0:T(8,128)(2,1)S(1)} %get-tuple-element.37), channel_id=1, source_target_pairs={{0,10},{1,11},{2,8},{3,9},{4,14},{5,15},{6,12},{7,13},{8,2},{9,3},... | collective-permute-start | bytes 196616 | tf_op jit(solution)/shard_map/ppermute | solution.py:136
  912.0 12.2 collective-permute-start.10
  913.6 11.8 collective-permute-start.11
  916.8 10.5 collective-permute-start.12
  918.7 9.4 collective-permute-start.13
  922.5 8.5 collective-permute-start.14
  924.2 9.4 collective-permute-start.15
  925.4 10.8 collective-permute-start.16
  927.3 10.2 collective-permute-start.17
  928.0 12.3 collective-permute-start.18
  931.0 10.5 collective-permute-start.19
  933.6 11.0 collective-permute-start.20
  936.3 10.0 collective-permute-start.21
  937.5 11.8 collective-permute-start.22
  940.3 10.8 collective-permute-start.23
  941.5 13.3 %collective-permute-start.24 = (bf16[1,2,64,256]{3,2,1,0:T(8,128)(2,1)}, bf16[1,2,64,256]{3,2,1,0:T(8,128)(2,1)S(1)}, u32[]{:S(2)}, u32[]{:S(2)}) collective-permute-start(bf16[1,2,64,256]{3,2,1,0:T(8,128)(2,1)} %get-tuple-element.54), channel_id=1, source_target_pairs={{0,10},{1,11},{2,8},{3,9},{4,14},{5,15},{6,12},{7,13},{8,2},{9,3},... | collective-permute-start | bytes 196616 | tf_op jit(solution)/shard_map/ppermute | solution.py:136
  944.5 12.2 collective-permute-start.25
  946.2 11.7 collective-permute-start.26
  949.3 10.7 collective-permute-start.27
  951.1 9.6 collective-permute-start.28
  954.8 10.3 collective-permute-start.29
  956.7 12.3 collective-permute-start.30
  957.9 13.4 %collective-permute-start.31 = (bf16[1,2,64,256]{3,2,1,0:T(8,128)(2,1)}, bf16[1,2,64,256]{3,2,1,0:T(8,128)(2,1)}, u32[]{:S(2)}, u32[]{:S(2)}) collective-permute-start(bf16[1,2,64,256]{3,2,1,0:T(8,128)(2,1)} %get-tuple-element.79), channel_id=1, source_target_pairs={{0,2},{1,3},{2,0},{3,1},{4,6},{5,7},{6,4},{7,5},{8,10},{9,11},{10,... | collective-permute-start | bytes 196616 | tf_op jit(solution)/shard_map/ppermute | solution.py:136
  960.1 14.6 %collective-permute-start.32 = (bf16[1,2,64,256]{3,2,1,0:T(8,128)(2,1)}, bf16[1,2,64,256]{3,2,1,0:T(8,128)(2,1)}, u32[]{:S(2)}, u32[]{:S(2)}) collective-permute-start(bf16[1,2,64,256]{3,2,1,0:T(8,128)(2,1)} %get-tuple-element.78), channel_id=1, source_target_pairs={{0,3},{1,2},{2,1},{3,0},{4,7},{5,6},{6,5},{7,4},{8,11},{9,10},{10,... | collective-permute-start | bytes 196616 | tf_op jit(solution)/shard_map/ppermute | solution.py:136
  960.7 17.6 %collective-permute-start.33 = (bf16[1,2,64,256]{3,2,1,0:T(8,128)(2,1)}, bf16[1,2,64,256]{3,2,1,0:T(8,128)(2,1)}, u32[]{:S(2)}, u32[]{:S(2)}) collective-permute-start(bf16[1,2,64,256]{3,2,1,0:T(8,128)(2,1)} %get-tuple-element.77), channel_id=1, source_target_pairs={{0,4},{1,5},{2,6},{3,7},{4,0},{5,1},{6,2},{7,3},{8,12},{9,13},{10,... | collective-permute-start | bytes 196616 | tf_op jit(solution)/shard_map/ppermute | solution.py:136
  965.1 15.1 %collective-permute-start.34 = (bf16[1,2,64,256]{3,2,1,0:T(8,128)(2,1)}, bf16[1,2,64,256]{3,2,1,0:T(8,128)(2,1)}, u32[]{:S(2)}, u32[]{:S(2)}) collective-permute-start(bf16[1,2,64,256]{3,2,1,0:T(8,128)(2,1)} %get-tuple-element.76), channel_id=1, source_target_pairs={{0,5},{1,4},{2,7},{3,6},{4,1},{5,0},{6,3},{7,2},{8,13},{9,12},{10,... | collective-permute-start | bytes 196616 | tf_op jit(solution)/shard_map/ppermute | solution.py:136
  969.0 13.8 %collective-permute-start.35 = (bf16[1,2,64,256]{3,2,1,0:T(8,128)(2,1)}, bf16[1,2,64,256]{3,2,1,0:T(8,128)(2,1)S(1)}, u32[]{:S(2)}, u32[]{:S(2)}) collective-permute-start(bf16[1,2,64,256]{3,2,1,0:T(8,128)(2,1)} %get-tuple-element.75), channel_id=1, source_target_pairs={{0,6},{1,7},{2,4},{3,5},{4,2},{5,3},{6,0},{7,1},{8,14},{9,15},{10,... | collective-permute-start | bytes 196616 | tf_op jit(solution)/shard_map/ppermute | solution.py:136
  971.3 14.6 %collective-permute-start.36 = (bf16[1,2,64,256]{3,2,1,0:T(8,128)(2,1)}, bf16[1,2,64,256]{3,2,1,0:T(8,128)(2,1)S(1)}, u32[]{:S(2)}, u32[]{:S(2)}) collective-permute-start(bf16[1,2,64,256]{3,2,1,0:T(8,128)(2,1)} %get-tuple-element.74), channel_id=1, source_target_pairs={{0,7},{1,6},{2,5},{3,4},{4,3},{5,2},{6,1},{7,0},{8,15},{9,14},{10,... | collective-permute-start | bytes 196616 | tf_op jit(solution)/shard_map/ppermute | solution.py:136
  974.7 13.6 %collective-permute-start.37 = (bf16[1,2,64,256]{3,2,1,0:T(8,128)(2,1)}, bf16[1,2,64,256]{3,2,1,0:T(8,128)(2,1)S(1)}, u32[]{:S(2)}, u32[]{:S(2)}) collective-permute-start(bf16[1,2,64,256]{3,2,1,0:T(8,128)(2,1)} %get-tuple-element.73), channel_id=1, source_target_pairs={{0,8},{1,9},{2,10},{3,11},{4,12},{5,13},{6,14},{7,15},{8,0},{9,1},... | collective-permute-start | bytes 196616 | tf_op jit(solution)/shard_map/ppermute | solution.py:136
  978.3 12.4 collective-permute-start.38
  980.2 13.4 %collective-permute-start.39 = (bf16[1,2,64,256]{3,2,1,0:T(8,128)(2,1)}, bf16[1,2,64,256]{3,2,1,0:T(8,128)(2,1)S(1)}, u32[]{:S(2)}, u32[]{:S(2)}) collective-permute-start(bf16[1,2,64,256]{3,2,1,0:T(8,128)(2,1)} %get-tuple-element.71), channel_id=1, source_target_pairs={{0,10},{1,11},{2,8},{3,9},{4,14},{5,15},{6,12},{7,13},{8,2},{9,3},... | collective-permute-start | bytes 196616 | tf_op jit(solution)/shard_map/ppermute | solution.py:136
  982.9 13.6 %collective-permute-start.40 = (bf16[1,2,64,256]{3,2,1,0:T(8,128)(2,1)}, bf16[1,2,64,256]{3,2,1,0:T(8,128)(2,1)S(1)}, u32[]{:S(2)}, u32[]{:S(2)}) collective-permute-start(bf16[1,2,64,256]{3,2,1,0:T(8,128)(2,1)} %get-tuple-element.70), channel_id=1, source_target_pairs={{0,11},{1,10},{2,9},{3,8},{4,15},{5,14},{6,13},{7,12},{8,3},{9,2},... | collective-permute-start | bytes 196616 | tf_op jit(solution)/shard_map/ppermute | solution.py:136
  985.9 11.5 collective-permute-start.41
  988.3 10.2 collective-permute-start.42
  990.7 9.5 collective-permute-start.43
  993.6 9.2 collective-permute-start.44
  996.5 12.1 collective-permute-start.45
  997.4 13.1 %collective-permute-start.46 = (bf16[1,2,64,256]{3,2,1,0:T(8,128)(2,1)}, bf16[1,2,64,256]{3,2,1,0:T(8,128)(2,1)}, u32[]{:S(2)}, u32[]{:S(2)}) collective-permute-start(bf16[1,2,64,256]{3,2,1,0:T(8,128)(2,1)} %get-tuple-element.96), channel_id=1, source_target_pairs={{0,2},{1,3},{2,0},{3,1},{4,6},{5,7},{6,4},{7,5},{8,10},{9,11},{10,... | collective-permute-start | bytes 196616 | tf_op jit(solution)/shard_map/ppermute | solution.py:136
  998.5 15.4 %collective-permute-start.47 = (bf16[1,2,64,256]{3,2,1,0:T(8,128)(2,1)}, bf16[1,2,64,256]{3,2,1,0:T(8,128)(2,1)}, u32[]{:S(2)}, u32[]{:S(2)}) collective-permute-start(bf16[1,2,64,256]{3,2,1,0:T(8,128)(2,1)} %get-tuple-element.95), channel_id=1, source_target_pairs={{0,3},{1,2},{2,1},{3,0},{4,7},{5,6},{6,5},{7,4},{8,11},{9,10},{10,... | collective-permute-start | bytes 196616 | tf_op jit(solution)/shard_map/ppermute | solution.py:136
  1000.2 17.1 %collective-permute-start.48 = (bf16[1,2,64,256]{3,2,1,0:T(8,128)(2,1)}, bf16[1,2,64,256]{3,2,1,0:T(8,128)(2,1)}, u32[]{:S(2)}, u32[]{:S(2)}) collective-permute-start(bf16[1,2,64,256]{3,2,1,0:T(8,128)(2,1)} %get-tuple-element.94), channel_id=1, source_target_pairs={{0,4},{1,5},{2,6},{3,7},{4,0},{5,1},{6,2},{7,3},{8,12},{9,13},{10,... | collective-permute-start | bytes 196616 | tf_op jit(solution)/shard_map/ppermute | solution.py:136
  1002.8 16.9 %collective-permute-start.49 = (bf16[1,2,64,256]{3,2,1,0:T(8,128)(2,1)}, bf16[1,2,64,256]{3,2,1,0:T(8,128)(2,1)}, u32[]{:S(2)}, u32[]{:S(2)}) collective-permute-start(bf16[1,2,64,256]{3,2,1,0:T(8,128)(2,1)} %get-tuple-element.93), channel_id=1, source_target_pairs={{0,5},{1,4},{2,7},{3,6},{4,1},{5,0},{6,3},{7,2},{8,13},{9,12},{10,... | collective-permute-start | bytes 196616 | tf_op jit(solution)/shard_map/ppermute | solution.py:136
  1008.5 13.8 %collective-permute-start.50 = (bf16[1,2,64,256]{3,2,1,0:T(8,128)(2,1)}, bf16[1,2,64,256]{3,2,1,0:T(8,128)(2,1)S(1)}, u32[]{:S(2)}, u32[]{:S(2)}) collective-permute-start(bf16[1,2,64,256]{3,2,1,0:T(8,128)(2,1)} %get-tuple-element.92), channel_id=1, source_target_pairs={{0,6},{1,7},{2,4},{3,5},{4,2},{5,3},{6,0},{7,1},{8,14},{9,15},{10,... | collective-permute-start | bytes 196616 | tf_op jit(solution)/shard_map/ppermute | solution.py:136
  1010.6 14.6 %collective-permute-start.51 = (bf16[1,2,64,256]{3,2,1,0:T(8,128)(2,1)}, bf16[1,2,64,256]{3,2,1,0:T(8,128)(2,1)S(1)}, u32[]{:S(2)}, u32[]{:S(2)}) collective-permute-start(bf16[1,2,64,256]{3,2,1,0:T(8,128)(2,1)} %get-tuple-element.91), channel_id=1, source_target_pairs={{0,7},{1,6},{2,5},{3,4},{4,3},{5,2},{6,1},{7,0},{8,15},{9,14},{10,... | collective-permute-start | bytes 196616 | tf_op jit(solution)/shard_map/ppermute | solution.py:136
  1013.9 13.8 %collective-permute-start.52 = (bf16[1,2,64,256]{3,2,1,0:T(8,128)(2,1)}, bf16[1,2,64,256]{3,2,1,0:T(8,128)(2,1)S(1)}, u32[]{:S(2)}, u32[]{:S(2)}) collective-permute-start(bf16[1,2,64,256]{3,2,1,0:T(8,128)(2,1)} %get-tuple-element.90), channel_id=1, source_target_pairs={{0,8},{1,9},{2,10},{3,11},{4,12},{5,13},{6,14},{7,15},{8,0},{9,1},... | collective-permute-start | bytes 196616 | tf_op jit(solution)/shard_map/ppermute | solution.py:136
  1017.4 12.8 collective-permute-start.53
  1019.7 13.7 %collective-permute-start.54 = (bf16[1,2,64,256]{3,2,1,0:T(8,128)(2,1)S(1)}, bf16[1,2,64,256]{3,2,1,0:T(8,128)(2,1)S(1)}, u32[]{:S(2)}, u32[]{:S(2)}) collective-permute-start(bf16[1,2,64,256]{3,2,1,0:T(8,128)(2,1)S(1)} %get-tuple-element.88), channel_id=1, source_target_pairs={{0,10},{1,11},{2,8},{3,9},{4,14},{5,15},{6,12},{7,13},{8,2},{9,3},... | collective-permute-start | bytes 196616 | tf_op jit(solution)/shard_map/ppermute | solution.py:136
  1022.3 13.4 %collective-permute-start.55 = (bf16[1,2,64,256]{3,2,1,0:T(8,128)(2,1)S(1)}, bf16[1,2,64,256]{3,2,1,0:T(8,128)(2,1)S(1)}, u32[]{:S(2)}, u32[]{:S(2)}) collective-permute-start(bf16[1,2,64,256]{3,2,1,0:T(8,128)(2,1)S(1)} %get-tuple-element.87), channel_id=1, source_target_pairs={{0,11},{1,10},{2,9},{3,8},{4,15},{5,14},{6,13},{7,12},{8,3},{9,2},... | collective-permute-start | bytes 196616 | tf_op jit(solution)/shard_map/ppermute | solution.py:136
  1025.2 11.2 collective-permute-start.56
  1027.7 9.3 collective-permute-start.57
  1030.2 7.4 collective-permute-start.58
  1033.5 14.7 %collective-permute-start.59 = (bf16[1,2,64,256]{3,2,1,0:T(8,128)(2,1)S(1)}, bf16[1,2,64,256]{3,2,1,0:T(8,128)(2,1)S(1)}, u32[]{:S(2)}, u32[]{:S(2)}) collective-permute-start(bf16[1,2,64,256]{3,2,1,0:T(8,128)(2,1)S(1)} %get-tuple-element.83), channel_id=1, source_target_pairs={{0,15},{1,14},{2,13},{3,12},{4,11},{5,10},{6,9},{7,8},{8,7},{9,6},... | collective-permute-start | bytes 196616 | tf_op jit(solution)/shard_map/ppermute | solution.py:136
  (15 other events, 176.4 us)
